TPU v7x, 256 devices: a whole 4x4x8 slice. The times are simulated.
256 devices in a mesh: blk: 128 (over z, x, y_hi, core), tm: 2 (over y_lo).
Axes of the slice: x: 4, y: 4 (y_hi: 2, y_lo: 2; y = y_hi * 2 + y_lo), z: 8, core: 2. Of those that a mesh axis runs over, the one named last changes fastest.
Arguments:
- history: bfloat16 [4, 32768, 512], P(None, 'blk', 'tm'), may hold values from -6 to 6
- panel_pos: bfloat16 [3, 32768], P(None, 'blk'), may hold values from -2 to 2, as said below
- area: bfloat16 [32768], P('blk'), may hold values from 0.5 to 2
- observer_pos: float32 [3, 131072], P(None, 'blk'), may hold values from -2 to 2, as said below
- delays: int32 [128, 7], P('blk'), may hold values from -64 to 64, as said below
Outputs:
- pressure: float32 [131072, 512], P('blk', 'tm')
Inputs may be any that keep to these rules, and one draw needn't show every extreme that they name: `delays`: -64 and 64 are both taken. `observer_pos`: the third coordinate (height) of every observer is 0.1 or more. `panel_pos`: the third coordinate (height) of every panel centre is 0 or less.
All inputs are finite; a program needn't handle non-finite values.
Results may differ from a plain program's by a relative error of at most 0.0034.
Values may be sent and summed in bfloat16 or wider, within the bound.
A program may use at most 128 MiB of HBM per device.

v0:
```python
import math

import jax
import jax.numpy as jnp
from jax import lax
from jax.sharding import PartitionSpec as P

MAXLAG = 64
HALF = 3


four_pi = 4.0 * math.pi


def from_behind(value, axis, steps):
    count = lax.axis_size(axis)
    pairs = [(source, (source + steps) % count) for source in range(count)]
    return lax.ppermute(value, axis, pairs)


def pair_weights(observers, positions, areas):
    apart = observers[:, :, None] - positions[:, None, :]
    distance = jnp.sqrt(jnp.sum(apart * apart, axis=0))
    inverse = 1.0 / distance
    scaled = areas[None, :] * inverse / four_pi
    loads_fast = scaled[None] * apart * inverse[None]
    loads_slow = loads_fast * inverse[None]
    stacked = jnp.stack(
        [
            scaled,
            loads_fast[0],
            loads_fast[1],
            loads_fast[2],
            loads_slow[0],
            loads_slow[1],
            loads_slow[2],
        ],
        axis=1,
    )
    return stacked.reshape(observers.shape[1], 7 * positions.shape[1]).astype(jnp.bfloat16)


def block_signal(source, first_index, sample_count):
    padded = jnp.pad(source, ((0, 0), (0, 0), (MAXLAG + 1, MAXLAG + 1)))
    segment = lax.dynamic_slice_in_dim(padded, first_index + MAXLAG, sample_count + 2, 2)
    values = segment[:, :, 1:-1].astype(jnp.float32)
    slopes = 0.5 * (segment[:, :, 2:].astype(jnp.float32) - segment[:, :, :-2].astype(jnp.float32))
    stacked = jnp.concatenate([slopes, values[1:]], axis=0).astype(jnp.bfloat16)
    return stacked.reshape(7 * source.shape[1], sample_count)


def per_device(history, panel_pos, area, observer_pos, delays):
    tm_index = lax.axis_index("tm")
    slice_width = history.shape[2]
    extended = lax.all_gather(history, "tm", axis=2, tiled=True)
    slice_start = tm_index * slice_width

    def contribute(block, column):
        source, positions, areas = block
        weights = pair_weights(
            observer_pos, positions.astype(jnp.float32), areas.astype(jnp.float32)
        )
        signals = block_signal(source, slice_start - delays[0, column], slice_width)
        return jnp.dot(weights, signals, preferred_element_type=jnp.float32)

    own_block = (extended, panel_pos, area)
    block = from_behind((own_block[0], own_block[1], own_block[2]), "blk", HALF)
    total = contribute(block, 0)
    for column in range(1, 2 * HALF + 1):
        block = from_behind((block[0], block[1], block[2]), "blk", -1)
        total = total + contribute(block, column)
    return total


def solution(mesh):
    return jax.shard_map(
        per_device,
        mesh=mesh,
        in_specs=(P(None, "blk", "tm"), P(None, "blk"), P("blk"), P(None, "blk"), P("blk", None)),
        out_specs=P("blk", "tm"),
        check_vma=False,
    )
```

profile of v0, /device:TPU:8, one launch (start us, length us, event | category | flops | bytes accessed | tf_op | source)
XLA Modules:
  0.0 270.4 jit_solution(10828807043325366926)
XLA Ops:
  8.3 7.2 %collective-permute-done = bf16[3,256]{1,0:T(4,128)(2,1)S(1)} collective-permute-done((bf16[3,256]{1,0:T(4,128)(2,1)}, bf16[3,256]{1,0:T(4,128)(2,1)S(1)}, u32[]{:S(2)}, u32[]{:S(2)}) %collective-permute-start) | collective-permute-done | bytes 1568 | tf_op jit(solution)/shard_map/ppermute | solution.py:18
  15.5 5.0 %collective-permute-start.3 = (bf16[3,256]{1,0:T(4,128)(2,1)S(1)}, bf16[3,256]{1,0:T(4,128)(2,1)S(1)}, u32[]{:S(2)}, u32[]{:S(2)}) collective-permute-start(bf16[3,256]{1,0:T(4,128)(2,1)S(1)} %collective-permute-done), channel_id=1, source_target_pairs={{0,254},{2,0},{4,2},{6,4},{8,6},{10,8},{12,10},{14,12},{16,14},{18... | collective-permute-start | bytes 4616 | tf_op jit(solution)/shard_map/ppermute | solution.py:18
  21.8 7.4 %collective-permute-start.6 = (bf16[3,256]{1,0:T(4,128)(2,1)S(1)}, bf16[3,256]{1,0:T(4,128)(2,1)S(1)}, u32[]{:S(2)}, u32[]{:S(2)}) collective-permute-start(bf16[3,256]{1,0:T(4,128)(2,1)S(1)} %collective-permute-done.3), channel_id=1, source_target_pairs={{0,254},{2,0},{4,2},{6,4},{8,6},{10,8},{12,10},{14,12},{16,14},{18... | collective-permute-start | bytes 4616 | tf_op jit(solution)/shard_map/ppermute | solution.py:18
  30.5 7.4 %collective-permute-start.9 = (bf16[3,256]{1,0:T(4,128)(2,1)S(1)}, bf16[3,256]{1,0:T(4,128)(2,1)S(1)}, u32[]{:S(2)}, u32[]{:S(2)}) collective-permute-start(bf16[3,256]{1,0:T(4,128)(2,1)S(1)} %collective-permute-done.6), channel_id=1, source_target_pairs={{0,254},{2,0},{4,2},{6,4},{8,6},{10,8},{12,10},{14,12},{16,14},{18... | collective-permute-start | bytes 4616 | tf_op jit(solution)/shard_map/ppermute | solution.py:18
  39.5 7.1 %collective-permute-start.12 = (bf16[3,256]{1,0:T(4,128)(2,1)S(1)}, bf16[3,256]{1,0:T(4,128)(2,1)S(1)}, u32[]{:S(2)}, u32[]{:S(2)}) collective-permute-start(bf16[3,256]{1,0:T(4,128)(2,1)S(1)} %collective-permute-done.9), channel_id=1, source_target_pairs={{0,254},{2,0},{4,2},{6,4},{8,6},{10,8},{12,10},{14,12},{16,14},{18... | collective-permute-start | bytes 4616 | tf_op jit(solution)/shard_map/ppermute | solution.py:18
  49.3 7.4 %collective-permute-start.7 = (bf16[256]{0:T(256)(128)(2,1)S(1)}, bf16[256]{0:T(256)(128)(2,1)S(1)}, u32[]{:S(2)}, u32[]{:S(2)}) collective-permute-start(bf16[256]{0:T(256)(128)(2,1)S(1)} %collective-permute-done.4), channel_id=1, source_target_pairs={{0,254},{2,0},{4,2},{6,4},{8,6},{10,8},{12,10},{14,12},{16,14},{18... | collective-permute-start | bytes 1544 | tf_op jit(solution)/shard_map/ppermute | solution.py:18
  58.0 7.4 %collective-permute-start.10 = (bf16[256]{0:T(256)(128)(2,1)S(1)}, bf16[256]{0:T(256)(128)(2,1)S(1)}, u32[]{:S(2)}, u32[]{:S(2)}) collective-permute-start(bf16[256]{0:T(256)(128)(2,1)S(1)} %collective-permute-done.7), channel_id=1, source_target_pairs={{0,254},{2,0},{4,2},{6,4},{8,6},{10,8},{12,10},{14,12},{16,14},{18... | collective-permute-start | bytes 1544 | tf_op jit(solution)/shard_map/ppermute | solution.py:18
  66.7 7.4 %collective-permute-start.13 = (bf16[256]{0:T(256)(128)(2,1)S(1)}, bf16[256]{0:T(256)(128)(2,1)S(1)}, u32[]{:S(2)}, u32[]{:S(2)}) collective-permute-start(bf16[256]{0:T(256)(128)(2,1)S(1)} %collective-permute-done.10), channel_id=1, source_target_pairs={{0,254},{2,0},{4,2},{6,4},{8,6},{10,8},{12,10},{14,12},{16,14},{18... | collective-permute-start | bytes 1544 | tf_op jit(solution)/shard_map/ppermute | solution.py:18
  75.4 7.4 %collective-permute-start.16 = (bf16[256]{0:T(256)(128)(2,1)S(1)}, bf16[256]{0:T(256)(128)(2,1)S(1)}, u32[]{:S(2)}, u32[]{:S(2)}) collective-permute-start(bf16[256]{0:T(256)(128)(2,1)S(1)} %collective-permute-done.13), channel_id=1, source_target_pairs={{0,254},{2,0},{4,2},{6,4},{8,6},{10,8},{12,10},{14,12},{16,14},{18... | collective-permute-start | bytes 1544 | tf_op jit(solution)/shard_map/ppermute | solution.py:18
  84.1 7.4 %collective-permute-start.19 = (bf16[256]{0:T(256)(128)(2,1)S(1)}, bf16[256]{0:T(256)(128)(2,1)S(1)}, u32[]{:S(2)}, u32[]{:S(2)}) collective-permute-start(bf16[256]{0:T(256)(128)(2,1)S(1)} %collective-permute-done.16), channel_id=1, source_target_pairs={{0,254},{2,0},{4,2},{6,4},{8,6},{10,8},{12,10},{14,12},{16,14},{18... | collective-permute-start | bytes 1544 | tf_op jit(solution)/shard_map/ppermute | solution.py:18
  103.7 6.4 %fusion.34 = (bf16[3,1024,256]{2,1,0:T(8,128)(2,1)S(1)}, bf16[3,1024,256]{2,1,0:T(8,128)(2,1)S(1)}, bf16[3,1024,256]{2,1,0:T(8,128)(2,1)S(1)}, bf16[3,1024,256]{...) fusion(f32[1024,256]{1,0:T(8,128)S(1)} %get-tuple-element.27, ...), kind=kLoop, calls=%fused_computation.48 | loop fusion | flops 28311552 | bytes 31488000 | tf_op jit(solution)/shard_map/convert.21
  128.4 14.4 %collective-permute-done.2 = bf16[4,256,512]{2,1,0:T(8,128)(2,1)S(1)} collective-permute-done((bf16[4,256,512]{2,1,0:T(8,128)(2,1)}, bf16[4,256,512]{2,1,0:T(8,128)(2,1)S(1)}, u32[]{:S(2)}, u32[]{:S(2)}) %collective-permute-start.2) | collective-permute-done | bytes 1048608 | tf_op jit(solution)/shard_map/ppermute | solution.py:18
  142.8 5.8 %collective-permute-start.5 = (bf16[4,256,512]{2,1,0:T(8,128)(2,1)S(1)}, bf16[4,256,512]{2,1,0:T(8,128)(2,1)S(1)}, u32[]{:S(2)}, u32[]{:S(2)}) collective-permute-start(bf16[4,256,512]{2,1,0:T(8,128)(2,1)S(1)} %collective-permute-done.2), channel_id=1, source_target_pairs={{0,254},{2,0},{4,2},{6,4},{8,6},{10,8},{12,10},{14,12},{16,14},{18... | collective-permute-start | bytes 3145736 | tf_op jit(solution)/shard_map/ppermute | solution.py:18
  150.9 10.0 %collective-permute-done.5 = bf16[4,256,512]{2,1,0:T(8,128)(2,1)S(1)} collective-permute-done((bf16[4,256,512]{2,1,0:T(8,128)(2,1)S(1)}, bf16[4,256,512]{2,1,0:T(8,128)(2,1)S(1)}, u32[]{:S(2)}, u32[]{:S(2)}) %collective-permute-start.5) | collective-permute-done | bytes 1048608 | tf_op jit(solution)/shard_map/ppermute | solution.py:18
  160.9 7.6 %collective-permute-start.8 = (bf16[4,256,512]{2,1,0:T(8,128)(2,1)S(1)}, bf16[4,256,512]{2,1,0:T(8,128)(2,1)S(1)}, u32[]{:S(2)}, u32[]{:S(2)}) collective-permute-start(bf16[4,256,512]{2,1,0:T(8,128)(2,1)S(1)} %collective-permute-done.5), channel_id=1, source_target_pairs={{0,254},{2,0},{4,2},{6,4},{8,6},{10,8},{12,10},{14,12},{16,14},{18... | collective-permute-start | bytes 3145736 | tf_op jit(solution)/shard_map/ppermute | solution.py:18
  169.4 11.5 %collective-permute-done.8 = bf16[4,256,512]{2,1,0:T(8,128)(2,1)S(1)} collective-permute-done((bf16[4,256,512]{2,1,0:T(8,128)(2,1)S(1)}, bf16[4,256,512]{2,1,0:T(8,128)(2,1)S(1)}, u32[]{:S(2)}, u32[]{:S(2)}) %collective-permute-start.8) | collective-permute-done | bytes 1048608 | tf_op jit(solution)/shard_map/ppermute | solution.py:18
  180.9 7.6 %collective-permute-start.11 = (bf16[4,256,512]{2,1,0:T(8,128)(2,1)S(1)}, bf16[4,256,512]{2,1,0:T(8,128)(2,1)S(1)}, u32[]{:S(2)}, u32[]{:S(2)}) collective-permute-start(bf16[4,256,512]{2,1,0:T(8,128)(2,1)S(1)} %collective-permute-done.8), channel_id=1, source_target_pairs={{0,254},{2,0},{4,2},{6,4},{8,6},{10,8},{12,10},{14,12},{16,14},{18... | collective-permute-start | bytes 3145736 | tf_op jit(solution)/shard_map/ppermute | solution.py:18
  189.5 11.4 %collective-permute-done.11 = bf16[4,256,512]{2,1,0:T(8,128)(2,1)S(1)} collective-permute-done((bf16[4,256,512]{2,1,0:T(8,128)(2,1)S(1)}, bf16[4,256,512]{2,1,0:T(8,128)(2,1)S(1)}, u32[]{:S(2)}, u32[]{:S(2)}) %collective-permute-start.11) | collective-permute-done | bytes 1048608 | tf_op jit(solution)/shard_map/ppermute | solution.py:18
  200.8 7.6 %collective-permute-start.14 = (bf16[4,256,512]{2,1,0:T(8,128)(2,1)S(1)}, bf16[4,256,512]{2,1,0:T(8,128)(2,1)S(1)}, u32[]{:S(2)}, u32[]{:S(2)}) collective-permute-start(bf16[4,256,512]{2,1,0:T(8,128)(2,1)S(1)} %collective-permute-done.11), channel_id=1, source_target_pairs={{0,254},{2,0},{4,2},{6,4},{8,6},{10,8},{12,10},{14,12},{16,14},{18... | collective-permute-start | bytes 3145736 | tf_op jit(solution)/shard_map/ppermute | solution.py:18
  214.3 6.5 %collective-permute-done.14 = bf16[4,256,512]{2,1,0:T(8,128)(2,1)S(1)} collective-permute-done((bf16[4,256,512]{2,1,0:T(8,128)(2,1)S(1)}, bf16[4,256,512]{2,1,0:T(8,128)(2,1)S(1)}, u32[]{:S(2)}, u32[]{:S(2)}) %collective-permute-start.14) | collective-permute-done | bytes 1048608 | tf_op jit(solution)/shard_map/ppermute | solution.py:18
  220.8 7.6 %collective-permute-start.17 = (bf16[4,256,512]{2,1,0:T(8,128)(2,1)S(1)}, bf16[4,256,512]{2,1,0:T(8,128)(2,1)S(1)}, u32[]{:S(2)}, u32[]{:S(2)}) collective-permute-start(bf16[4,256,512]{2,1,0:T(8,128)(2,1)S(1)} %collective-permute-done.14), channel_id=1, source_target_pairs={{0,254},{2,0},{4,2},{6,4},{8,6},{10,8},{12,10},{14,12},{16,14},{18... | collective-permute-start | bytes 3145736 | tf_op jit(solution)/shard_map/ppermute | solution.py:18
  232.4 8.4 %collective-permute-done.17 = bf16[4,256,512]{2,1,0:T(8,128)(2,1)S(1)} collective-permute-done((bf16[4,256,512]{2,1,0:T(8,128)(2,1)S(1)}, bf16[4,256,512]{2,1,0:T(8,128)(2,1)S(1)}, u32[]{:S(2)}, u32[]{:S(2)}) %collective-permute-start.17) | collective-permute-done | bytes 1048608 | tf_op jit(solution)/shard_map/ppermute | solution.py:18
  240.7 7.6 %collective-permute-start.20 = (bf16[4,256,512]{2,1,0:T(8,128)(2,1)S(1)}, bf16[4,256,512]{2,1,0:T(8,128)(2,1)S(1)}, u32[]{:S(2)}, u32[]{:S(2)}) collective-permute-start(bf16[4,256,512]{2,1,0:T(8,128)(2,1)S(1)} %collective-permute-done.17), channel_id=1, source_target_pairs={{0,254},{2,0},{4,2},{6,4},{8,6},{10,8},{12,10},{14,12},{16,14},{18... | collective-permute-start | bytes 3145736 | tf_op jit(solution)/shard_map/ppermute | solution.py:18
  251.4 9.3 %collective-permute-done.20 = bf16[4,256,512]{2,1,0:T(8,128)(2,1)S(1)} collective-permute-done((bf16[4,256,512]{2,1,0:T(8,128)(2,1)S(1)}, bf16[4,256,512]{2,1,0:T(8,128)(2,1)S(1)}, u32[]{:S(2)}, u32[]{:S(2)}) %collective-permute-start.20) | collective-permute-done | bytes 1048608 | tf_op jit(solution)/shard_map/ppermute | solution.py:18
  (137 shorter events, 59.2 us)
Async XLA Ops:
  6.5 118.5 %all-gather.2.cloned.1.call-start = ((), (), s32[]{:S(2)}) async-start(), calls=%async_computation | async-start | bytes 1572864 | tf_op jit(solution)/shard_map/all_gather | solution.py:55
  6.5 9.0 %collective-permute-start = (bf16[3,256]{1,0:T(4,128)(2,1)}, bf16[3,256]{1,0:T(4,128)(2,1)S(1)}, u32[]{:S(2)}, u32[]{:S(2)}) collective-permute-start(bf16[3,256]{1,0:T(4,128)(2,1)} %param.6), channel_id=1, source_target_pairs={{0,6},{2,8},{4,10},{6,12},{8,14},{10,16},{12,18},{14,20},{16,22},{... | collective-permute-start | bytes 4616 | tf_op jit(solution)/shard_map/ppermute | solution.py:18
  15.5 6.3 %collective-permute-start.3 = (bf16[3,256]{1,0:T(4,128)(2,1)S(1)}, bf16[3,256]{1,0:T(4,128)(2,1)S(1)}, u32[]{:S(2)}, u32[]{:S(2)}) collective-permute-start(bf16[3,256]{1,0:T(4,128)(2,1)S(1)} %collective-permute-done), channel_id=1, source_target_pairs={{0,254},{2,0},{4,2},{6,4},{8,6},{10,8},{12,10},{14,12},{16,14},{18... | collective-permute-start | bytes 4616 | tf_op jit(solution)/shard_map/ppermute | solution.py:18
  21.8 8.7 %collective-permute-start.6 = (bf16[3,256]{1,0:T(4,128)(2,1)S(1)}, bf16[3,256]{1,0:T(4,128)(2,1)S(1)}, u32[]{:S(2)}, u32[]{:S(2)}) collective-permute-start(bf16[3,256]{1,0:T(4,128)(2,1)S(1)} %collective-permute-done.3), channel_id=1, source_target_pairs={{0,254},{2,0},{4,2},{6,4},{8,6},{10,8},{12,10},{14,12},{16,14},{18... | collective-permute-start | bytes 4616 | tf_op jit(solution)/shard_map/ppermute | solution.py:18
  29.2 18.7 %collective-permute-start.1 = (bf16[256]{0:T(256)(128)(2,1)}, bf16[256]{0:T(256)(128)(2,1)S(1)}, u32[]{:S(2)}, u32[]{:S(2)}) collective-permute-start(bf16[256]{0:T(256)(128)(2,1)} %param.7), channel_id=1, source_target_pairs={{0,6},{2,8},{4,10},{6,12},{8,14},{10,16},{12,18},{14,20},{16,22},{... | collective-permute-start | bytes 1544 | tf_op jit(solution)/shard_map/ppermute | solution.py:18
  30.5 9.0 %collective-permute-start.9 = (bf16[3,256]{1,0:T(4,128)(2,1)S(1)}, bf16[3,256]{1,0:T(4,128)(2,1)S(1)}, u32[]{:S(2)}, u32[]{:S(2)}) collective-permute-start(bf16[3,256]{1,0:T(4,128)(2,1)S(1)} %collective-permute-done.6), channel_id=1, source_target_pairs={{0,254},{2,0},{4,2},{6,4},{8,6},{10,8},{12,10},{14,12},{16,14},{18... | collective-permute-start | bytes 4616 | tf_op jit(solution)/shard_map/ppermute | solution.py:18
  39.5 17.1 %collective-permute-start.12 = (bf16[3,256]{1,0:T(4,128)(2,1)S(1)}, bf16[3,256]{1,0:T(4,128)(2,1)S(1)}, u32[]{:S(2)}, u32[]{:S(2)}) collective-permute-start(bf16[3,256]{1,0:T(4,128)(2,1)S(1)} %collective-permute-done.9), channel_id=1, source_target_pairs={{0,254},{2,0},{4,2},{6,4},{8,6},{10,8},{12,10},{14,12},{16,14},{18... | collective-permute-start | bytes 4616 | tf_op jit(solution)/shard_map/ppermute | solution.py:18
  47.9 1.4 collective-permute-start.4
  49.3 8.7 %collective-permute-start.7 = (bf16[256]{0:T(256)(128)(2,1)S(1)}, bf16[256]{0:T(256)(128)(2,1)S(1)}, u32[]{:S(2)}, u32[]{:S(2)}) collective-permute-start(bf16[256]{0:T(256)(128)(2,1)S(1)} %collective-permute-done.4), channel_id=1, source_target_pairs={{0,254},{2,0},{4,2},{6,4},{8,6},{10,8},{12,10},{14,12},{16,14},{18... | collective-permute-start | bytes 1544 | tf_op jit(solution)/shard_map/ppermute | solution.py:18
  56.7 18.0 %collective-permute-start.15 = (bf16[3,256]{1,0:T(4,128)(2,1)S(1)}, bf16[3,256]{1,0:T(4,128)(2,1)S(1)}, u32[]{:S(2)}, u32[]{:S(2)}) collective-permute-start(bf16[3,256]{1,0:T(4,128)(2,1)S(1)} %collective-permute-done.12), channel_id=1, source_target_pairs={{0,254},{2,0},{4,2},{6,4},{8,6},{10,8},{12,10},{14,12},{16,14},{18... | collective-permute-start | bytes 4616 | tf_op jit(solution)/shard_map/ppermute | solution.py:18
  58.0 8.7 %collective-permute-start.10 = (bf16[256]{0:T(256)(128)(2,1)S(1)}, bf16[256]{0:T(256)(128)(2,1)S(1)}, u32[]{:S(2)}, u32[]{:S(2)}) collective-permute-start(bf16[256]{0:T(256)(128)(2,1)S(1)} %collective-permute-done.7), channel_id=1, source_target_pairs={{0,254},{2,0},{4,2},{6,4},{8,6},{10,8},{12,10},{14,12},{16,14},{18... | collective-permute-start | bytes 1544 | tf_op jit(solution)/shard_map/ppermute | solution.py:18
  66.7 8.7 %collective-permute-start.13 = (bf16[256]{0:T(256)(128)(2,1)S(1)}, bf16[256]{0:T(256)(128)(2,1)S(1)}, u32[]{:S(2)}, u32[]{:S(2)}) collective-permute-start(bf16[256]{0:T(256)(128)(2,1)S(1)} %collective-permute-done.10), channel_id=1, source_target_pairs={{0,254},{2,0},{4,2},{6,4},{8,6},{10,8},{12,10},{14,12},{16,14},{18... | collective-permute-start | bytes 1544 | tf_op jit(solution)/shard_map/ppermute | solution.py:18
  74.7 18.1 %collective-permute-start.18 = (bf16[3,256]{1,0:T(4,128)(2,1)S(1)}, bf16[3,256]{1,0:T(4,128)(2,1)S(1)}, u32[]{:S(2)}, u32[]{:S(2)}) collective-permute-start(bf16[3,256]{1,0:T(4,128)(2,1)S(1)} %collective-permute-done.15), channel_id=1, source_target_pairs={{0,254},{2,0},{4,2},{6,4},{8,6},{10,8},{12,10},{14,12},{16,14},{18... | collective-permute-start | bytes 4616 | tf_op jit(solution)/shard_map/ppermute | solution.py:18
  75.4 8.7 %collective-permute-start.16 = (bf16[256]{0:T(256)(128)(2,1)S(1)}, bf16[256]{0:T(256)(128)(2,1)S(1)}, u32[]{:S(2)}, u32[]{:S(2)}) collective-permute-start(bf16[256]{0:T(256)(128)(2,1)S(1)} %collective-permute-done.13), channel_id=1, source_target_pairs={{0,254},{2,0},{4,2},{6,4},{8,6},{10,8},{12,10},{14,12},{16,14},{18... | collective-permute-start | bytes 1544 | tf_op jit(solution)/shard_map/ppermute | solution.py:18
  84.1 8.7 %collective-permute-start.19 = (bf16[256]{0:T(256)(128)(2,1)S(1)}, bf16[256]{0:T(256)(128)(2,1)S(1)}, u32[]{:S(2)}, u32[]{:S(2)}) collective-permute-start(bf16[256]{0:T(256)(128)(2,1)S(1)} %collective-permute-done.16), channel_id=1, source_target_pairs={{0,254},{2,0},{4,2},{6,4},{8,6},{10,8},{12,10},{14,12},{16,14},{18... | collective-permute-start | bytes 1544 | tf_op jit(solution)/shard_map/ppermute | solution.py:18
  125.0 23.6 %copy-start = (bf16[3,1024,256]{2,1,0:T(8,128)(2,1)S(1)}, bf16[3,1024,256]{2,1,0:T(8,128)(2,1)}, u32[]{:S(2)}) copy-start(bf16[3,1024,256]{2,1,0:T(8,128)(2,1)} %get-tuple-element.43) | copy-start | bytes 4718596
  125.0 17.8 %collective-permute-start.2 = (bf16[4,256,512]{2,1,0:T(8,128)(2,1)}, bf16[4,256,512]{2,1,0:T(8,128)(2,1)S(1)}, u32[]{:S(2)}, u32[]{:S(2)}) collective-permute-start(bf16[4,256,512]{2,1,0:T(8,128)(2,1)} %all-gather.2.cloned.1.call-done), channel_id=1, source_target_pairs={{0,6},{2,8},{4,10},{6,12},{8,14},{10,16},{12,18},{14,20},{16,22},{... | collective-permute-start | bytes 3145736 | tf_op jit(solution)/shard_map/ppermute | solution.py:18
  142.8 18.1 %collective-permute-start.5 = (bf16[4,256,512]{2,1,0:T(8,128)(2,1)S(1)}, bf16[4,256,512]{2,1,0:T(8,128)(2,1)S(1)}, u32[]{:S(2)}, u32[]{:S(2)}) collective-permute-start(bf16[4,256,512]{2,1,0:T(8,128)(2,1)S(1)} %collective-permute-done.2), channel_id=1, source_target_pairs={{0,254},{2,0},{4,2},{6,4},{8,6},{10,8},{12,10},{14,12},{16,14},{18... | collective-permute-start | bytes 3145736 | tf_op jit(solution)/shard_map/ppermute | solution.py:18
  160.9 19.9 %collective-permute-start.8 = (bf16[4,256,512]{2,1,0:T(8,128)(2,1)S(1)}, bf16[4,256,512]{2,1,0:T(8,128)(2,1)S(1)}, u32[]{:S(2)}, u32[]{:S(2)}) collective-permute-start(bf16[4,256,512]{2,1,0:T(8,128)(2,1)S(1)} %collective-permute-done.5), channel_id=1, source_target_pairs={{0,254},{2,0},{4,2},{6,4},{8,6},{10,8},{12,10},{14,12},{16,14},{18... | collective-permute-start | bytes 3145736 | tf_op jit(solution)/shard_map/ppermute | solution.py:18
  180.9 19.9 %collective-permute-start.11 = (bf16[4,256,512]{2,1,0:T(8,128)(2,1)S(1)}, bf16[4,256,512]{2,1,0:T(8,128)(2,1)S(1)}, u32[]{:S(2)}, u32[]{:S(2)}) collective-permute-start(bf16[4,256,512]{2,1,0:T(8,128)(2,1)S(1)} %collective-permute-done.8), channel_id=1, source_target_pairs={{0,254},{2,0},{4,2},{6,4},{8,6},{10,8},{12,10},{14,12},{16,14},{18... | collective-permute-start | bytes 3145736 | tf_op jit(solution)/shard_map/ppermute | solution.py:18
  200.8 19.9 %collective-permute-start.14 = (bf16[4,256,512]{2,1,0:T(8,128)(2,1)S(1)}, bf16[4,256,512]{2,1,0:T(8,128)(2,1)S(1)}, u32[]{:S(2)}, u32[]{:S(2)}) collective-permute-start(bf16[4,256,512]{2,1,0:T(8,128)(2,1)S(1)} %collective-permute-done.11), channel_id=1, source_target_pairs={{0,254},{2,0},{4,2},{6,4},{8,6},{10,8},{12,10},{14,12},{16,14},{18... | collective-permute-start | bytes 3145736 | tf_op jit(solution)/shard_map/ppermute | solution.py:18
  220.8 19.9 %collective-permute-start.17 = (bf16[4,256,512]{2,1,0:T(8,128)(2,1)S(1)}, bf16[4,256,512]{2,1,0:T(8,128)(2,1)S(1)}, u32[]{:S(2)}, u32[]{:S(2)}) collective-permute-start(bf16[4,256,512]{2,1,0:T(8,128)(2,1)S(1)} %collective-permute-done.14), channel_id=1, source_target_pairs={{0,254},{2,0},{4,2},{6,4},{8,6},{10,8},{12,10},{14,12},{16,14},{18... | collective-permute-start | bytes 3145736 | tf_op jit(solution)/shard_map/ppermute | solution.py:18
  230.5 17.9 %copy-start.10 = (bf16[1024,7,256]{2,0,1:T(8,128)(2,1)S(1)}, bf16[1024,7,256]{2,0,1:T(8,128)(2,1)}, u32[]{:S(2)}) copy-start(bf16[1024,7,256]{2,0,1:T(8,128)(2,1)} %fusion.95) | copy-start | bytes 11010052
  240.7 19.9 %collective-permute-start.20 = (bf16[4,256,512]{2,1,0:T(8,128)(2,1)S(1)}, bf16[4,256,512]{2,1,0:T(8,128)(2,1)S(1)}, u32[]{:S(2)}, u32[]{:S(2)}) collective-permute-start(bf16[4,256,512]{2,1,0:T(8,128)(2,1)S(1)} %collective-permute-done.17), channel_id=1, source_target_pairs={{0,254},{2,0},{4,2},{6,4},{8,6},{10,8},{12,10},{14,12},{16,14},{18... | collective-permute-start | bytes 3145736 | tf_op jit(solution)/shard_map/ppermute | solution.py:18
  (10 other events, 63.8 us)
Sparse Core Ops, SparseCore 0:
  29.4 21.9 all-gather.1
where the time goes:
time: 271 us; the launch traced here: 270 us
  starting transfers between devices  110 us (41%)
  waiting for transfers between devices  85.5 us (32%)
  local copies, waits for them, and re-layouts  23.4 us (9%)
  other arithmetic  22.5 us (8%)
  between operations  18.3 us (7%)
  matrix products  10.8 us (4%)
    ppermute x21, starting transfers between devices, from_behind(): return lax.ppermute(value, axis, pairs)  110 us
    ppermute x21, waiting for transfers between devices, from_behind(): return lax.ppermute(value, axis, pairs)  85.5 us
    unnamed x58, local copies, waits for them, and re-layouts  18.5 us
    another operation x9, other arithmetic  11.1 us
    dot_general x7, matrix products, contribute(): return jnp.dot(weights, signals, preferred_element_type=jnp.float32)  10.8 us
  transfers between devices with their start and end apart: 22, of which 16 were waited for; matrix products, arithmetic and copies ran while one was open for 20% of the time, Pallas kernels for 0%

commit v1 on v0

v1 whole, which is shorter than its diff:
```python
import functools
import math

import jax
import jax.numpy as jnp
from jax import lax
from jax.experimental import pallas as pl
from jax.experimental.pallas import tpu as pltpu
from jax.sharding import PartitionSpec as P

MESH = pl.DeviceIdType.MESH
MAIN, HALO = 256, 80
EXT = MAIN + HALO
STAGE = HALO + MAIN + HALO
COEF = 7
INV_FOUR_PI = 1.0 / (4.0 * math.pi)
OWN, SIB, ACROSS, SIDE, SIB_ACROSS, RELAY, SIB_RELAY = range(7)
HEAD, GEOM = 4, 5


def kernel(history, place, area, observers, delays, out,
           ext, geom, weights, signals, stage, spread,
           send_sem, recv_sem, halo_send, halo_recv):
    g = lax.axis_index("blk")
    half = lax.axis_index("tm")
    blocks = lax.axis_size("blk")
    core = g % 2
    upper = (g // 2) % 2
    sign = 1 - 2 * upper
    inner = (core + upper) % 2
    sibling = g + 1 - 2 * core
    across = g + 2 * sign
    ahead = (g + 4 * sign + blocks) % blocks
    behind = (g - 4 * sign + blocks) % blocks
    beside = (sibling + 4 * sign * (2 * inner - 1) + blocks) % blocks
    target = {SIB: sibling, ACROSS: across, SIDE: beside, SIB_ACROSS: sibling, RELAY: ahead, SIB_RELAY: sibling}
    origin = {SIB: OWN, ACROSS: OWN, SIDE: OWN, SIB_ACROSS: ACROSS, RELAY: ACROSS, SIB_RELAY: RELAY}
    slot = {OWN: 3, SIB: 4 - 2 * inner, ACROSS: 5, SIDE: 6 * inner, SIB_ACROSS: 6 - 2 * inner, RELAY: 1,
            SIB_RELAY: 2 - 2 * inner}

    barrier = pltpu.get_barrier_semaphore()
    for device in (sibling, across, ahead, behind, beside):
        pl.semaphore_signal(barrier, inc=1, device_id=(device, half), device_id_type=MESH)
    pl.semaphore_signal(barrier, inc=1, device_id=(g, 1 - half), device_id_type=MESH)

    geom[OWN] = jnp.zeros((8, 256), jnp.float32)
    geom[OWN, 0:3, :] = place[...].astype(jnp.float32)
    geom[OWN, 3:4, :] = area[...].astype(jnp.float32) * INV_FOUR_PI

    def flip(c):
        ext[OWN, c, 0:MAIN, :] = history[c].T

    def copy(edge, part):
        source, dest = origin[edge], edge
        if part == GEOM:
            src, dst = geom.at[source], geom.at[dest]
        elif part == HEAD:
            src, dst = ext.at[source, 0, pl.ds(MAIN, HALO)], ext.at[dest, 0, pl.ds(MAIN, HALO)]
        elif part == 0 and source == OWN:
            src, dst = ext.at[source, 0, pl.ds(0, MAIN)], ext.at[dest, 0, pl.ds(0, MAIN)]
        else:
            src, dst = ext.at[source, part], ext.at[dest, part]
        return pltpu.make_async_remote_copy(
            src_ref=src, dst_ref=dst, send_sem=send_sem.at[edge - 1, part], recv_sem=recv_sem.at[edge - 1, part],
            device_id=(target[edge], half), device_id_type=MESH)

    def halo(c):
        first = pl.multiple_of((MAIN - HALO) * (1 - half), 16)
        return pltpu.make_async_remote_copy(
            src_ref=ext.at[OWN, c, pl.ds(first, HALO)], dst_ref=ext.at[OWN, c, pl.ds(MAIN, HALO)],
            send_sem=halo_send.at[c], recv_sem=halo_recv.at[c], device_id=(g, 1 - half), device_id_type=MESH)

    def fill_weights(buf):
        @pl.loop(0, 32)
        def _(i):
            rows = pl.ds(pl.multiple_of(i * 32, 32), 32)
            for lane in (0, 128):
                cols = pl.ds(lane, 128)
                dx = spread[0, rows, :] - geom[buf, 0:1, cols]
                dy = spread[1, rows, :] - geom[buf, 1:2, cols]
                dz = spread[2, rows, :] - geom[buf, 2:3, cols]
                inv = lax.rsqrt(dx * dx + dy * dy + dz * dz)
                s = geom[buf, 3:4, cols] * inv
                fast = s * inv
                slow = fast * inv
                for n, value in enumerate((s, fast * dx, fast * dy, fast * dz, slow * dx, slow * dy, slow * dz)):
                    weights[buf, rows, pl.ds(n * 256 + lane, 128)] = value.astype(jnp.bfloat16)

    def delay_of(buf):
        m = slot[buf]
        return delays[0, m + upper * (6 - 2 * m)]

    def fill_signals(buf, c):
        k = delay_of(buf)
        edge = ext[buf, c, MAIN:EXT, :].astype(jnp.float32)
        zero = jnp.zeros_like(edge)
        late = half == 1
        for lane in (0, 1):
            cols = slice(lane * 128, lane * 128 + 128)
            stage[lane, 0:HALO, :] = jnp.where(late, edge, zero)[:, cols]
            stage[lane, HALO:HALO + MAIN, :] = ext[buf, c, 0:MAIN, cols].astype(jnp.float32)
            stage[lane, HALO + MAIN:STAGE, :] = jnp.where(late, zero, edge)[:, cols]
            after = stage[lane, pl.ds(HALO + 1 - k, MAIN), :]
            before = stage[lane, pl.ds(HALO - 1 - k, MAIN), :]
            at = c * 256 + lane * 128
            signals[:, at:at + 128] = (0.5 * (after - before)).astype(jnp.bfloat16)
            if c:
                signals[:, at + 768:at + 896] = stage[lane, pl.ds(HALO - k, MAIN), :].astype(jnp.bfloat16)

    def multiply(buf, first):
        @pl.loop(0, 2)
        def _(i):
            rows = pl.ds(pl.multiple_of(i * 512, 512), 512)
            part = lax.dot_general(weights[buf, rows, :], signals[...], (((1,), (1,)), ((), ())),
                                   preferred_element_type=jnp.float32)
            if first:
                out[rows, :] = part
            else:
                out[rows, :] += part

    def contribute(buf, first=False):
        for c in range(4):
            fill_signals(buf, c)
        multiply(buf, first)

    mine = (ACROSS, SIDE, SIB)
    flip(0)
    pl.semaphore_wait(barrier, 6)
    for edge in mine:
        copy(edge, GEOM).start()
    halo(0).start()
    for edge in mine:
        copy(edge, 0).start()
    for c in range(1, 4):
        flip(c)
        halo(c).start()
    for axis in range(3):
        for i in range(8):
            line = observers[axis:axis + 1, i * 128:(i + 1) * 128]
            spread[axis, i * 128:(i + 1) * 128, :] = jnp.broadcast_to(line, (128, 128)).T
    halo(0).wait_recv()
    for edge in mine:
        copy(edge, HEAD).start()
    for c in range(1, 4):
        halo(c).wait_recv()
        for edge in mine:
            copy(edge, c).start()

    def arrived(edge, part):
        copy(edge, part).wait_recv()
        if part == 0 and origin[edge] == OWN:
            copy(edge, HEAD).wait_recv()

    def relay(edge, part):
        arrived(edge, part)
        if edge == ACROSS:
            copy(RELAY, part).start()
            copy(SIB_ACROSS, part).start()
        else:
            copy(SIB_RELAY, part).start()

    fill_weights(OWN)
    relay(ACROSS, GEOM)
    copy(SIB, GEOM).wait_recv()
    fill_weights(SIB)
    copy(SIDE, GEOM).wait_recv()
    fill_weights(SIDE)
    fill_weights(ACROSS)
    relay(ACROSS, 0)
    copy(SIB_ACROSS, GEOM).wait_recv()
    fill_weights(SIB_ACROSS)
    contribute(OWN, True)
    relay(ACROSS, 1)
    relay(RELAY, GEOM)
    fill_weights(RELAY)
    copy(SIB_RELAY, GEOM).wait_recv()
    fill_weights(SIB_RELAY)
    relay(ACROSS, 2)
    for c in range(4):
        arrived(SIB, c)
    contribute(SIB)
    relay(RELAY, 0)
    relay(ACROSS, 3)
    for c in range(4):
        arrived(SIDE, c)
    contribute(SIDE)
    relay(RELAY, 1)
    contribute(ACROSS)
    for c in range(4):
        arrived(SIB_ACROSS, c)
    contribute(SIB_ACROSS)
    relay(RELAY, 2)
    relay(RELAY, 3)
    contribute(RELAY)
    for c in range(4):
        arrived(SIB_RELAY, c)
    contribute(SIB_RELAY)

    for c in range(4):
        halo(c).wait_send()
    for edge in target:
        for part in range(6):
            if part != HEAD or origin[edge] == OWN:
                copy(edge, part).wait_send()


def per_device(history, panel_pos, area, observer_pos, delays):
    vmem = pl.BlockSpec(memory_space=pltpu.VMEM)
    return pl.pallas_call(
        kernel,
        out_shape=jax.ShapeDtypeStruct((1024, 256), jnp.float32),
        in_specs=[vmem, vmem, vmem, vmem, pl.BlockSpec(memory_space=pltpu.SMEM)],
        out_specs=vmem,
        scratch_shapes=[
            pltpu.VMEM((7, 4, EXT, 256), jnp.bfloat16),
            pltpu.VMEM((7, 8, 256), jnp.float32),
            pltpu.VMEM((7, 1024, COEF * 256), jnp.bfloat16),
            pltpu.VMEM((256, COEF * 256), jnp.bfloat16),
            pltpu.VMEM((2, STAGE, 128), jnp.float32),
            pltpu.VMEM((3, 1024, 128), jnp.float32),
            pltpu.SemaphoreType.DMA((6, 6)),
            pltpu.SemaphoreType.DMA((6, 6)),
            pltpu.SemaphoreType.DMA((4,)),
            pltpu.SemaphoreType.DMA((4,)),
        ],
        compiler_params=pltpu.CompilerParams(
            collective_id=0, has_side_effects=True, vmem_limit_bytes=56 * 1024 * 1024),
        cost_estimate=pl.CostEstimate(flops=6_580_000_000, bytes_accessed=2_000_000, transcendentals=1_900_000),
    )(history, panel_pos, area.reshape(1, 256), observer_pos, delays)


def solution(mesh):
    return jax.shard_map(
        per_device,
        mesh=mesh,
        in_specs=(P(None, "blk", "tm"), P(None, "blk"), P("blk"), P(None, "blk"), P("blk", None)),
        out_specs=P("blk", "tm"),
        check_vma=False,
    )
```

time: 271 us -> 49.6 us (0.18)
  the two profiles are of different devices: /device:TPU:8 before, /device:TPU:1 now
where the time goes in v1:
time: 49.6 us; the launch traced here: 49.5 us
  Pallas kernels  46 us (93%)
  local copies, waits for them, and re-layouts  3.48 us (7%)
    pallas_call x1, Pallas kernels, per_device(): pl.pallas_call(kernel, out_shape=jax.ShapeDtypeStruct((1024, 256), jnp.fl...  46 us
    unnamed x1, local copies, waits for them, and re-layouts  2.26 us
    reshape x1, local copies, waits for them, and re-layouts, per_device(): area.reshape(1, 256)  1.22 us

profile of v1, /device:TPU:1, one launch (start us, length us, event | category | flops | bytes accessed | tf_op | source)
XLA Modules:
  0.0 49.5 jit_solution(5687701886274043588)
XLA Ops:
  0.0 1.2 %reshape.3.area = bf16[1,256]{1,0:T(2,128)(2,1)} reshape(bf16[256]{0:T(256)(128)(2,1)} %param.7) | data formatting | bytes 1024 | tf_op jit(solution)/shard_map/reshape | solution.py:229
  1.2 46.0 %shard_map.55 = f32[1024,256]{1,0:T(8,128)} custom-call(bf16[4,256,256]{2,1,0:T(8,128)(2,1)} %history.1, bf16[3,256]{1,0:T(4,128)(2,1)} %place.1, bf16[1,256]{1,0:T(2,128)(2,1)} %reshape.3.area, f32[3,1024]{1,0:T(4,128)} %observers.1, s32[1,7]{1,0:T(1,128)} %delays.1), custom_call_target="tpu_custom_call" | custom-call | flops 6579999744 | bytes 2000000 | tf_op jit(solution)/shard_map/pallas_call | solution.py:209
  47.2 2.3 %copy.7 = f32[1024,256]{1,0:T(8,128)} copy(f32[1024,256]{1,0:T(8,128)} %shard_map.55) | data formatting | bytes 2097152

commit v2 on v1

v2 whole, which is shorter than its diff:
```python
import math

import jax
import jax.numpy as jnp
from jax import lax
from jax.experimental import pallas as pl
from jax.experimental.pallas import tpu as pltpu
from jax.sharding import PartitionSpec as P

MESH = pl.DeviceIdType.MESH
MAIN, HALO = 256, 80
BODY = MAIN - HALO
EXT = MAIN + HALO
STAGE = HALO + MAIN + HALO
COEF = 7
INV_FOUR_PI = 1.0 / (4.0 * math.pi)
OWN, SIB, ACROSS, SIDE, SIB_ACROSS, RELAY, SIB_RELAY = range(7)
EDGE, OUTER, GEOM = 4, 5, 6


def kernel(history, place, area, observers, delays, out,
           ext, geom, weights, signals, stage, spread, lags, send_sem, recv_sem):
    g = lax.axis_index("blk")
    half = lax.axis_index("tm")
    blocks = lax.axis_size("blk")
    core = g % 2
    upper = (g // 2) % 2
    sign = 1 - 2 * upper
    inner = (core + upper) % 2
    sibling = g + 1 - 2 * core
    across = g + 2 * sign
    ahead = (g + 4 * sign + blocks) % blocks
    behind = (g - 4 * sign + blocks) % blocks
    beside = (sibling + 4 * sign * (2 * inner - 1) + blocks) % blocks
    facing = g + inner * sign
    target = {SIB: sibling, ACROSS: across, SIDE: beside, SIB_ACROSS: sibling, RELAY: ahead, SIB_RELAY: sibling}
    origin = {SIB: OWN, ACROSS: OWN, SIDE: OWN, SIB_ACROSS: ACROSS, RELAY: ACROSS, SIB_RELAY: RELAY}
    slot = {OWN: 3, SIB: 4 - 2 * inner, ACROSS: 5, SIDE: 6 * inner, SIB_ACROSS: 6 - 2 * inner, RELAY: 1,
            SIB_RELAY: 2 - 2 * inner}
    edge_rows = pl.ds(pl.multiple_of(BODY * (1 - half), 16), HALO)
    body_rows = pl.ds(pl.multiple_of(HALO * half, 16), BODY)
    outer_rows = pl.ds(MAIN, HALO)

    barrier = pltpu.get_barrier_semaphore()
    for device, part in ((sibling, half), (across, half), (ahead, half), (behind, half), (beside, half),
                         (g, 1 - half), (across, 1 - half), (facing, 1 - half)):
        pl.semaphore_signal(barrier, inc=1, device_id=(device, part), device_id_type=MESH)

    geom[OWN] = jnp.zeros((8, 256), jnp.float32)
    geom[OWN, 0:3, :] = place[...].astype(jnp.float32)
    geom[OWN, 3:4, :] = area[...].astype(jnp.float32).reshape(1, 256) * INV_FOUR_PI
    for buf, m in slot.items():
        lags[buf] = delays[0, m + upper * (6 - 2 * m)]

    def flip(c):
        ext[OWN, c, 0:MAIN, :] = history[c].T

    def view(buf, part):
        if part == GEOM:
            return geom.at[buf]
        if part == EDGE:
            return ext.at[buf, :, edge_rows]
        if part == OUTER:
            return ext.at[buf, :, outer_rows]
        return ext.at[buf, part, body_rows]

    def copy(buf, part):
        if part == OUTER and buf in (OWN, ACROSS, RELAY):
            source = {OWN: OWN, ACROSS: OWN, RELAY: RELAY - (RELAY - SIDE) * inner}[buf]
            device = {OWN: g, ACROSS: across, RELAY: facing}[buf]
            src, where = view(source, EDGE), (device, 1 - half)
        else:
            src, where = view(origin[buf], part), (target[buf], half)
        return pltpu.make_async_remote_copy(
            src_ref=src, dst_ref=view(buf, part), send_sem=send_sem.at[buf, part], recv_sem=recv_sem.at[buf, part],
            device_id=where, device_id_type=MESH)

    def fill_weights(buf):
        @pl.loop(0, 16, unroll=4)
        def _(i):
            rows = pl.ds(pl.multiple_of(i * 64, 64), 64)
            ox, oy, oz = (spread[n, rows, :] for n in range(3))
            for lane in (0, 128):
                cols = pl.ds(lane, 128)
                dx = ox - geom[buf, 0:1, cols]
                dy = oy - geom[buf, 1:2, cols]
                dz = oz - geom[buf, 2:3, cols]
                inv = lax.rsqrt(dx * dx + dy * dy + dz * dz)
                s = geom[buf, 3:4, cols] * inv
                fast = s * inv
                fx, fy, fz = fast * dx, fast * dy, fast * dz
                for n, value in enumerate((s, fx, fx * inv, fy, fy * inv, fz, fz * inv)):
                    weights[buf, rows, pl.ds(n * 256 + lane, 128)] = value.astype(jnp.bfloat16)

    def fill_signals(buf, c):
        k = lags[buf]
        edge = ext[buf, c, MAIN:EXT, :].astype(jnp.float32)
        zero = jnp.zeros_like(edge)
        late = half == 1
        for lane in (0, 1):
            cols = slice(lane * 128, lane * 128 + 128)
            stage[lane, 0:HALO, :] = jnp.where(late, edge, zero)[:, cols]
            stage[lane, HALO:HALO + MAIN, :] = ext[buf, c, 0:MAIN, cols].astype(jnp.float32)
            stage[lane, HALO + MAIN:STAGE, :] = jnp.where(late, zero, edge)[:, cols]
            after = stage[lane, pl.ds(HALO + 1 - k, MAIN), :]
            before = stage[lane, pl.ds(HALO - 1 - k, MAIN), :]
            at = max(2 * c - 1, 0) * 256 + lane * 128
            signals[at:at + 128, :] = (0.5 * (after - before)).astype(jnp.bfloat16).T
            if c:
                signals[at + 256:at + 384, :] = stage[lane, pl.ds(HALO - k, MAIN), :].astype(jnp.bfloat16).T

    def contribute(buf, channels=(0, 1, 2, 3), first=False):
        for c in channels:
            fill_signals(buf, c)
        cols = slice(max(2 * channels[0] - 1, 0) * 256, (2 * channels[-1] + 1) * 256)
        part = jnp.dot(weights[buf, :, cols], signals[cols, :], preferred_element_type=jnp.float32)
        if first:
            out[...] = part
        else:
            out[...] += part

    def arrived(buf, *parts):
        for part in parts:
            copy(buf, part).wait_recv()

    def send(part, *bufs):
        for buf in bufs:
            copy(buf, part).start()

    def relay(buf, part):
        arrived(buf, part)
        if buf == RELAY:
            send(part, SIB_RELAY)
        elif part == OUTER:
            send(part, SIB_ACROSS)
        else:
            send(part, RELAY, SIB_ACROSS)

    flip(0)
    pl.semaphore_wait(barrier, 8)
    send(GEOM, ACROSS, SIDE, SIB)
    send(0, ACROSS, SIDE, SIB)
    flip(1)
    send(1, ACROSS, SIDE, SIB)
    flip(2)
    flip(3)
    send(EDGE, ACROSS, SIDE)
    send(OUTER, OWN, ACROSS)
    send(2, ACROSS, SIDE)
    send(3, ACROSS, SIDE)
    send(EDGE, SIB)
    send(2, SIB)
    send(3, SIB)
    for axis in range(3):
        for i in range(8):
            line = observers[axis:axis + 1, i * 128:(i + 1) * 128]
            spread[axis, i * 128:(i + 1) * 128, :] = jnp.broadcast_to(line, (128, 128)).T

    fill_weights(OWN)
    relay(ACROSS, GEOM)
    arrived(SIB, GEOM)
    fill_weights(SIB)
    relay(ACROSS, 0)
    arrived(SIDE, GEOM)
    fill_weights(SIDE)
    relay(ACROSS, 1)
    fill_weights(ACROSS)
    arrived(SIB_ACROSS, GEOM)
    fill_weights(SIB_ACROSS)
    relay(ACROSS, EDGE)
    relay(RELAY, GEOM)
    arrived(OWN, OUTER)
    send(OUTER, SIDE, SIB)
    fill_weights(RELAY)
    relay(RELAY, 0)
    relay(ACROSS, OUTER)
    contribute(OWN, first=True)
    relay(ACROSS, 2)
    arrived(SIB_RELAY, GEOM)
    fill_weights(SIB_RELAY)
    relay(RELAY, 1)
    arrived(SIB, 0, 1, EDGE, OUTER, 2, 3)
    contribute(SIB)
    relay(ACROSS, 3)
    relay(RELAY, EDGE)
    arrived(SIDE, 0, 1, EDGE, 2, 3)
    send(OUTER, RELAY)
    arrived(SIDE, OUTER)
    contribute(SIDE)
    relay(RELAY, 2)
    contribute(ACROSS)
    relay(RELAY, OUTER)
    arrived(SIB_ACROSS, 0, 1, EDGE, OUTER, 2, 3)
    contribute(SIB_ACROSS)
    relay(RELAY, 3)
    contribute(RELAY)
    arrived(SIB_RELAY, 0, 1, EDGE, OUTER, 2, 3)
    contribute(SIB_RELAY)

    for buf in range(7):
        for part in range(7):
            if buf != OWN or part == OUTER:
                copy(buf, part).wait_send()


def per_device(history, panel_pos, area, observer_pos, delays):
    vmem = pl.BlockSpec(memory_space=pltpu.VMEM)
    return pl.pallas_call(
        kernel,
        out_shape=jax.ShapeDtypeStruct((1024, 256), jnp.float32),
        in_specs=[vmem, vmem, vmem, vmem, pl.BlockSpec(memory_space=pltpu.SMEM)],
        out_specs=vmem,
        scratch_shapes=[
            pltpu.VMEM((7, 4, EXT, 256), jnp.bfloat16),
            pltpu.VMEM((7, 8, 256), jnp.float32),
            pltpu.VMEM((7, 1024, COEF * 256), jnp.bfloat16),
            pltpu.VMEM((COEF * 256, 256), jnp.bfloat16),
            pltpu.VMEM((2, STAGE, 128), jnp.float32),
            pltpu.VMEM((3, 1024, 128), jnp.float32),
            pltpu.SMEM((8,), jnp.int32),
            pltpu.SemaphoreType.DMA((7, 7)),
            pltpu.SemaphoreType.DMA((7, 7)),
        ],
        compiler_params=pltpu.CompilerParams(
            collective_id=0, has_side_effects=True, vmem_limit_bytes=56 * 1024 * 1024),
        cost_estimate=pl.CostEstimate(flops=6_580_000_000, bytes_accessed=2_000_000, transcendentals=1_900_000),
    )(history, panel_pos, area, observer_pos, delays)


def solution(mesh):
    return jax.shard_map(
        per_device,
        mesh=mesh,
        in_specs=(P(None, "blk", "tm"), P(None, "blk"), P("blk"), P(None, "blk"), P("blk", None)),
        out_specs=P("blk", "tm"),
        check_vma=False,
    )
```

time: 49.6 us -> 46.4 us (0.935)
  Pallas kernels: 46 us -> 44 us
  local copies, waits for them, and re-layouts: 3.48 us -> 2.26 us
    pallas_call x1, Pallas kernels: 46 us -> 44 us  [per_device(): pl.pallas_call(kernel, out_shape=jax.ShapeDtypeStruct((1024, 256), jnp.fl...]
    reshape x1 -> x0, local copies, waits for them, and re-layouts: 1.22 us -> none  [per_device(): area.reshape(1, 256)]
where the time goes in v2:
time: 46.4 us; the launch traced here: 46.2 us
  Pallas kernels  44 us (95%)
  local copies, waits for them, and re-layouts  2.26 us (5%)
    pallas_call x1, Pallas kernels, per_device(): pl.pallas_call(kernel, out_shape=jax.ShapeDtypeStruct((1024, 256), jnp.fl...  44 us
    unnamed x1, local copies, waits for them, and re-layouts  2.26 us

profile of v2, /device:TPU:1, one launch (start us, length us, event | category | flops | bytes accessed | tf_op | source)
XLA Modules:
  0.0 46.2 jit_solution(16316106785758651038)
XLA Ops:
  0.0 44.0 %shard_map.55 = f32[1024,256]{1,0:T(8,128)} custom-call(bf16[4,256,256]{2,1,0:T(8,128)(2,1)} %history.1, bf16[3,256]{1,0:T(4,128)(2,1)} %place.1, bf16[256]{0:T(256)(128)(2,1)} %area.1, f32[3,1024]{1,0:T(4,128)} %observers.1, s32[1,7]{1,0:T(1,128)} %delays.1), custom_call_target="tpu_custom_call" | custom-call | flops 6579999744 | bytes 2000000 | tf_op jit(solution)/shard_map/pallas_call | solution.py:208
  44.0 2.3 %copy.7 = f32[1024,256]{1,0:T(8,128)} copy(f32[1024,256]{1,0:T(8,128)} %shard_map.55) | data formatting | bytes 2097152

commit v3 on v2

--- a/solution.py
+++ b/solution.py
@@ -174,28 +174,41 @@
     fill_weights(RELAY)
     relay(RELAY, 0)
     relay(ACROSS, OUTER)
-    contribute(OWN, first=True)
     relay(ACROSS, 2)
     arrived(SIB_RELAY, GEOM)
     fill_weights(SIB_RELAY)
     relay(RELAY, 1)
-    arrived(SIB, 0, 1, EDGE, OUTER, 2, 3)
-    contribute(SIB)
     relay(ACROSS, 3)
-    relay(RELAY, EDGE)
-    arrived(SIDE, 0, 1, EDGE, 2, 3)
-    send(OUTER, RELAY)
-    arrived(SIDE, OUTER)
-    contribute(SIDE)
-    relay(RELAY, 2)
-    contribute(ACROSS)
-    relay(RELAY, OUTER)
-    arrived(SIB_ACROSS, 0, 1, EDGE, OUTER, 2, 3)
-    contribute(SIB_ACROSS)
-    relay(RELAY, 3)
-    contribute(RELAY)
-    arrived(SIB_RELAY, 0, 1, EDGE, OUTER, 2, 3)
-    contribute(SIB_RELAY)
+    out[...] = jnp.zeros_like(out)
+
+    @pl.loop(0, 7)
+    def _(buf):
+        @pl.when(buf == SIB)
+        def _():
+            arrived(SIB, 0, 1, EDGE, OUTER, 2, 3)
+            relay(RELAY, EDGE)
+            arrived(SIDE, 0, 1, EDGE, 2, 3)
+            send(OUTER, RELAY)
+
+        @pl.when(buf == SIDE)
+        def _():
+            arrived(SIDE, OUTER)
+            arrived(SIB_ACROSS, 0, 1, EDGE, OUTER, 2, 3)
+
+        @pl.when(buf == ACROSS)
+        def _():
+            relay(RELAY, 2)
+
+        @pl.when(buf == SIB_ACROSS)
+        def _():
+            relay(RELAY, OUTER)
+            relay(RELAY, 3)
+
+        @pl.when(buf == SIB_RELAY)
+        def _():
+            arrived(SIB_RELAY, 0, 1, EDGE, OUTER, 2, 3)
+
+        contribute(buf)
 
     for buf in range(7):
         for part in range(7):

time: 46.4 us -> 43.4 us (0.935)
  Pallas kernels: 44 us -> 41 us
    pallas_call x1, Pallas kernels: 44 us -> 41 us  [per_device(): pl.pallas_call(kernel, out_shape=jax.ShapeDtypeStruct((1024, 256), jnp.fl...]
where the time goes in v3:
time: 43.4 us; the launch traced here: 43.3 us
  Pallas kernels  41 us (94%)
  local copies, waits for them, and re-layouts  2.26 us (5%)
    pallas_call x1, Pallas kernels, per_device(): pl.pallas_call(kernel, out_shape=jax.ShapeDtypeStruct((1024, 256), jnp.fl...  41 us
    unnamed x1, local copies, waits for them, and re-layouts  2.26 us

profile of v3, /device:TPU:1, one launch (start us, length us, event | category | flops | bytes accessed | tf_op | source)
XLA Modules:
  0.0 43.3 jit_solution(11621306125620067877)
XLA Ops:
  0.0 41.0 %shard_map.55 = f32[1024,256]{1,0:T(8,128)} custom-call(bf16[4,256,256]{2,1,0:T(8,128)(2,1)} %history.1, bf16[3,256]{1,0:T(4,128)(2,1)} %place.1, bf16[256]{0:T(256)(128)(2,1)} %area.1, f32[3,1024]{1,0:T(4,128)} %observers.1, s32[1,7]{1,0:T(1,128)} %delays.1), custom_call_target="tpu_custom_call" | custom-call | flops 6579999744 | bytes 2000000 | tf_op jit(solution)/shard_map/pallas_call | solution.py:221
  41.0 2.3 %copy.7 = f32[1024,256]{1,0:T(8,128)} copy(f32[1024,256]{1,0:T(8,128)} %shard_map.55) | data formatting | bytes 2097152

commit v4 on v3

--- a/solution.py
+++ b/solution.py
@@ -136,6 +136,10 @@
         else:
             send(part, RELAY, SIB_ACROSS)
 
+    for axis in range(3):
+        for i in range(8):
+            line = observers[axis:axis + 1, i * 128:(i + 1) * 128]
+            spread[axis, i * 128:(i + 1) * 128, :] = jnp.broadcast_to(line, (128, 128)).T
     flip(0)
     pl.semaphore_wait(barrier, 8)
     send(GEOM, ACROSS, SIDE, SIB)
@@ -151,10 +155,6 @@
     send(EDGE, SIB)
     send(2, SIB)
     send(3, SIB)
-    for axis in range(3):
-        for i in range(8):
-            line = observers[axis:axis + 1, i * 128:(i + 1) * 128]
-            spread[axis, i * 128:(i + 1) * 128, :] = jnp.broadcast_to(line, (128, 128)).T
 
     fill_weights(OWN)
     relay(ACROSS, GEOM)

time: 43.4 us -> 43.4 us (level)
  no operation moved by 1% of the time
where the time goes in v4:
time: 43.4 us; the launch traced here: 43.3 us
  Pallas kernels  41 us (94%)
  local copies, waits for them, and re-layouts  2.26 us (5%)
    pallas_call x1, Pallas kernels, per_device(): pl.pallas_call(kernel, out_shape=jax.ShapeDtypeStruct((1024, 256), jnp.fl...  41 us
    unnamed x1, local copies, waits for them, and re-layouts  2.26 us

profile of v4, /device:TPU:1, one launch (start us, length us, event | category | flops | bytes accessed | tf_op | source)
XLA Modules:
  0.0 43.3 jit_solution(5439317465793657179)
XLA Ops:
  0.0 41.0 %shard_map.55 = f32[1024,256]{1,0:T(8,128)} custom-call(bf16[4,256,256]{2,1,0:T(8,128)(2,1)} %history.1, bf16[3,256]{1,0:T(4,128)(2,1)} %place.1, bf16[256]{0:T(256)(128)(2,1)} %area.1, f32[3,1024]{1,0:T(4,128)} %observers.1, s32[1,7]{1,0:T(1,128)} %delays.1), custom_call_target="tpu_custom_call" | custom-call | flops 6579999744 | bytes 2000000 | tf_op jit(solution)/shard_map/pallas_call | solution.py:221
  41.0 2.3 %copy.7 = f32[1024,256]{1,0:T(8,128)} copy(f32[1024,256]{1,0:T(8,128)} %shard_map.55) | data formatting | bytes 2097152

commit v5 on v3

--- a/solution.py
+++ b/solution.py
@@ -202,6 +202,9 @@
         @pl.when(buf == SIB_ACROSS)
         def _():
             relay(RELAY, OUTER)
+
+        @pl.when(buf == RELAY)
+        def _():
             relay(RELAY, 3)
 
         @pl.when(buf == SIB_RELAY)

time: 43.4 us -> 43.8 us (level)
  no operation moved by 1% of the time
where the time goes in v5:
time: 43.8 us; the launch traced here: 43.7 us
  Pallas kernels  41.4 us (95%)
  local copies, waits for them, and re-layouts  2.26 us (5%)
    pallas_call x1, Pallas kernels, per_device(): pl.pallas_call(kernel, out_shape=jax.ShapeDtypeStruct((1024, 256), jnp.fl...  41.4 us
    unnamed x1, local copies, waits for them, and re-layouts  2.26 us

profile of v5, /device:TPU:1, one launch (start us, length us, event | category | flops | bytes accessed | tf_op | source)
XLA Modules:
  0.0 43.7 jit_solution(2474307937531359913)
XLA Ops:
  0.0 41.4 %shard_map.55 = f32[1024,256]{1,0:T(8,128)} custom-call(bf16[4,256,256]{2,1,0:T(8,128)(2,1)} %history.1, bf16[3,256]{1,0:T(4,128)(2,1)} %place.1, bf16[256]{0:T(256)(128)(2,1)} %area.1, f32[3,1024]{1,0:T(4,128)} %observers.1, s32[1,7]{1,0:T(1,128)} %delays.1), custom_call_target="tpu_custom_call" | custom-call | flops 6579999744 | bytes 2000000 | tf_op jit(solution)/shard_map/pallas_call | solution.py:224
  41.4 2.3 %copy.7 = f32[1024,256]{1,0:T(8,128)} copy(f32[1024,256]{1,0:T(8,128)} %shard_map.55) | data formatting | bytes 2097152
